TPU v7x, 512 devices: a whole 4x8x8 slice. The times are simulated.
512 devices in a mesh: grp: 8 (over y_lo, core), tile: 64 (over y_hi, x, z).
Axes of the slice: x: 4, y: 8 (y_hi: 2, y_lo: 4; y = y_hi * 4 + y_lo), z: 8, core: 2. Of those that a mesh axis runs over, the one named last changes fastest.
Arguments:
- hidden: bfloat16 [8, 512, 128, 128], P('grp', 'tile'), may hold values from -13 to 13
- cotangent: float32 [8, 512, 128], P('grp', 'tile'), may hold values from -16 to 16
- spectral_w: bfloat16 [4096, 256], P('tile'), may hold values from -0.375 to 0.375
- conv_k: float32 [9, 128], replicated, may hold values from -2 to 2
- proj_w: float32 [128], replicated, may hold values from -0.5 to 0.5
Outputs:
- grad_hidden: float32 [8, 512, 128, 128], P('grp', 'tile')
- grad_spectral: float32 [4096, 256], P('tile')
- grad_conv: float32 [9, 128], replicated
- grad_proj: float32 [128], replicated
All inputs are finite; a program needn't handle non-finite values.
Results may differ from a plain program's by a relative error of at most 0.015.
Values may be sent and summed in bfloat16 or wider, within the bound.
No kernel may reach another device: no remote copies, remote signals or barrier semaphores. Data moves between devices by JAX's collectives and lax.ppermute only.
A program may use at most 64 MiB of HBM per device.

v0:
```python
import jax
import jax.numpy as jnp
from jax import lax
from jax.sharding import PartitionSpec as P

HIGH = lax.Precision.HIGHEST


def padded(block, sides, width):
    for axis, dim in sides:
        count = lax.axis_size(axis)
        forward = [(i, i + 1) for i in range(count - 1)]
        backward = [(target, source) for source, target in forward]
        low = lax.ppermute(
            lax.slice_in_dim(block, block.shape[dim] - width, None, axis=dim), axis, forward
        )
        high = lax.ppermute(lax.slice_in_dim(block, 0, width, axis=dim), axis, backward)
        block = jnp.concatenate([low, block, high], axis=dim)
    return block


def spectral_tables(modes, bins):
    mode_idx = jnp.arange(modes, dtype=jnp.int32)
    bin_idx = jnp.arange(bins, dtype=jnp.int32)
    phase_int = mode_idx[:, None] * bin_idx[None, :] % bins
    angle_val = phase_int.astype(jnp.float32) * (2.0 * jnp.pi / bins)
    cosine = jnp.cos(angle_val)
    sine = jnp.sin(angle_val)
    forward_tab = jnp.concatenate([cosine, -sine], 0).astype(jnp.bfloat16)
    weight_k = jnp.where(mode_idx == 0, 1.0, 2.0).astype(jnp.float32)[:, None] / bins
    inverse_tab = jnp.concatenate([cosine * weight_k, -sine * weight_k], 0).T.astype(jnp.bfloat16)
    return (forward_tab, inverse_tab)


def build_mixer(weights, modes, chans):
    real_w = weights[:, :chans].reshape(modes, chans, chans)
    imag_w = weights[:, chans:].reshape(modes, chans, chans)
    upper = jnp.concatenate([real_w, imag_w], 2)
    lower = jnp.concatenate([-imag_w, real_w], 2)
    return jnp.concatenate([upper, lower], 1)


def gelu_pair(value):
    normal_cdf = 0.5 * (1.0 + jax.scipy.special.erf(value * 0.7071067811865476))
    return (
        value * normal_cdf,
        normal_cdf + value * jnp.exp(-0.5 * value * value) * 0.3989422804014327,
    )


def cell_backward(hidden_cells, local_term, cot_cells, mixer, forward_tab, inverse_tab, proj_w):
    modes = mixer.shape[0]
    chans = proj_w.shape[0]
    spec_h = jnp.einsum(
        "jb,pbc->jpc", forward_tab, hidden_cells, preferred_element_type=jnp.float32
    ).astype(jnp.bfloat16)
    h_cat = jnp.concatenate([spec_h[:modes], spec_h[modes:]], 2)
    mixed = jnp.einsum("kpa,kab->kpb", h_cat, mixer, preferred_element_type=jnp.float32).astype(
        jnp.bfloat16
    )
    mixed_stack = jnp.concatenate([mixed[:, :, :chans], mixed[:, :, chans:]], 0)
    spectral_out = jnp.einsum(
        "bj,jpo->pbo", inverse_tab, mixed_stack, preferred_element_type=jnp.float32
    )
    pre_act = spectral_out + local_term
    activ, slope = gelu_pair(pre_act)
    proj_grad = jnp.einsum("pb,pbo->o", cot_cells, activ, precision=HIGH)
    grad_pre = (cot_cells[:, :, None] * proj_w * slope).astype(jnp.bfloat16)
    grad_mix = jnp.einsum(
        "bj,pbo->jpo", inverse_tab, grad_pre, preferred_element_type=jnp.float32
    ).astype(jnp.bfloat16)
    grad_real = grad_mix[:modes]
    grad_imag = grad_mix[modes:]
    grad_cat = jnp.concatenate([grad_real, grad_imag], 2)
    grad_spec = jnp.einsum(
        "kpb,kab->kpa", grad_cat, mixer, preferred_element_type=jnp.float32
    ).astype(jnp.bfloat16)
    grad_stack = jnp.concatenate([grad_spec[:, :, :chans], grad_spec[:, :, chans:]], 0)
    grad_in = jnp.einsum("jb,jpc->pbc", forward_tab, grad_stack, preferred_element_type=jnp.float32)
    left_side = jnp.concatenate([spec_h[:modes], spec_h[modes:]], 1)
    right_side = jnp.concatenate([grad_cat, jnp.concatenate([grad_imag, -grad_real], 2)], 1)
    weight_term = jnp.einsum(
        "kpc,kpo->kco", left_side, right_side, preferred_element_type=jnp.float32
    ).reshape(modes * chans, 2 * chans)
    return (grad_pre, grad_in, weight_term, proj_grad)


def local(hidden, cotangent, spectral_w, conv_k, proj_w):
    rows_here, cols_here, bins_here, chans = hidden.shape
    modes = spectral_w.shape[0] * lax.axis_size("tile") // chans
    cell_count = rows_here * cols_here
    forward_tab, inverse_tab = spectral_tables(modes, bins_here)
    x_pad = padded(hidden, (("grp", 0), ("tile", 1)), 1)
    offsets = [(row_off, col_off) for row_off in (-1, 0, 1) for col_off in (-1, 0, 1)]
    local_term = jnp.zeros((rows_here, cols_here, bins_here, chans), jnp.float32)
    for index_d, (row_off, col_off) in enumerate(offsets):
        window = x_pad[1 + row_off : 1 + row_off + rows_here, 1 + col_off : 1 + col_off + cols_here]
        local_term = local_term + window.astype(jnp.float32) * conv_k[index_d]
    whole_w = lax.all_gather(spectral_w, "tile", axis=0, tiled=True)
    mixer = build_mixer(whole_w, modes, chans)
    grad_pre, grad_in, weight_term, proj_grad = cell_backward(
        hidden.reshape(cell_count, bins_here, chans),
        local_term.reshape(cell_count, bins_here, chans),
        cotangent.reshape(cell_count, bins_here),
        mixer,
        forward_tab,
        inverse_tab,
        proj_w,
    )
    grad_block = grad_pre.reshape(rows_here, cols_here, bins_here, chans)
    conv_part = jnp.stack(
        [
            jnp.einsum(
                "xybc,xybc->c",
                x_pad[1 + row_off : 1 + row_off + rows_here, 1 + col_off : 1 + col_off + cols_here],
                grad_block,
                preferred_element_type=jnp.float32,
            )
            for row_off, col_off in offsets
        ],
        0,
    )
    grad_pad = padded(grad_block, (("grp", 0), ("tile", 1)), 1)
    grad_hidden = grad_in.reshape(rows_here, cols_here, bins_here, chans)
    for index_d, (row_off, col_off) in enumerate(offsets):
        window = grad_pad[
            1 - row_off : 1 - row_off + rows_here, 1 - col_off : 1 - col_off + cols_here
        ]
        grad_hidden = grad_hidden + window.astype(jnp.float32) * conv_k[index_d]
    tile_share = lax.psum_scatter(weight_term, "tile", scatter_dimension=0, tiled=True)
    grad_spectral = lax.psum(tile_share.astype(jnp.bfloat16), "grp").astype(jnp.float32)
    conv_all, proj_all = lax.psum((conv_part, proj_grad), ("grp", "tile"))
    return (grad_hidden, grad_spectral, conv_all, proj_all)


def solution(mesh):
    in_specs = (P("grp", "tile", None, None), P("grp", "tile", None), P("tile", None), P(), P())
    out_specs = (P("grp", "tile", None, None), P("tile", None), P(), P())
    return jax.shard_map(local, mesh=mesh, in_specs=in_specs, out_specs=out_specs, check_vma=False)
```

profile of v0, /device:TPU:1, one launch (start us, length us, event | category | flops | bytes accessed | tf_op | source)
XLA Modules:
  0.0 639.4 jit_solution(11236863667525213482)
XLA Ops:
  7.9 1.1 copy.11
  9.1 8.8 %collective-permute-start.1 = (bf16[1,8,128,128]{2,3,1,0:T(8,128)(2,1)S(1)}, bf16[1,8,128,128]{2,3,1,0:T(8,128)(2,1)S(1)}, u32[]{:S(2)}, u32[]{:S(2)}) collective-permute-start(bf16[1,8,128,128]{2,3,1,0:T(8,128)(2,1)S(1)} %copy.11), channel_id=1, source_target_pairs={{64,0},{128,64},{192,128},{256,192},{320,256},{384,320},{448,384},... | collective-permute-start | bytes 786440 | tf_op jit(solution)/shard_map/ppermute | solution.py:17
  17.9 1.9 collective-permute-start
  19.9 1.1 convolution_convert_fusion.1
  21.1 1.0 slice_bitcast_fusion.8
  23.1 1.3 collective-permute-start.3
  24.4 4.0 collective-permute-start.2
  28.4 119.3 %all-gather.2.cloned.1.call-done = bf16[4096,256]{1,0:T(8,128)(2,1)} async-done(((bf16[64,256]{1,0:T(8,128)(2,1)}), bf16[4096,256]{1,0:T(8,128)(2,1)}) %all-gather.2.cloned.1.call-update) | async-done | bytes 2097168 | tf_op jit(solution)/shard_map/all_gather | solution.py:99
  147.7 1.7 fusion.52
  150.9 1.6 bitcast_convert_fusion
  152.8 2.7 fusion.24
  155.5 6.4 %collective-permute-start.5 = (bf16[1,8,128,128]{2,3,1,0:T(8,128)(2,1)S(1)}, bf16[1,8,128,128]{2,3,1,0:T(8,128)(2,1)}, u32[]{:S(2)}, u32[]{:S(2)}) collective-permute-start(bf16[1,8,128,128]{2,3,1,0:T(8,128)(2,1)S(1)} %bitcast.128), channel_id=1, source_target_pairs={{64,0},{128,64},{192,128},{256,192},{320,256},{384,320},{448,384},... | collective-permute-start | bytes 786440 | tf_op jit(solution)/shard_map/ppermute | solution.py:17
  161.9 5.1 collective-permute-start.4
  167.4 1.0 fusion.14
  168.4 1.2 fusion.15
  169.7 3.2 fusion.3
  173.5 97.4 %all-reduce = (f32[9,128]{1,0:T(8,128)}, f32[128]{0:T(128)}) all-reduce(f32[9,128]{1,0:T(8,128)S(1)} %stack.39, f32[128]{0:T(128)S(1)} %convolution_bitcast_fusion.2), channel_id=1, replica_groups=mesh['grp'=8,'tile'=64] {'grp','tile'}, use_global_device_ids=true, to_apply=%region_2.3 | all-reduce | flops 1280 | bytes 10240 | tf_op jit(solution)/shard_map/psum | solution.py:132
  271.8 1.3 collective-permute-start.6
  273.1 4.0 collective-permute-start.7
  277.5 1.3 collective-permute-done.7
  278.9 2.1 fusion.21
  281.1 1.0 copy.20
  282.1 273.8 %reduce-scatter.2.cloned.1.call-done = f32[64,256]{1,0:T(8,128)} async-done(((f32[4096,256]{1,0:T(8,128)}), f32[64,256]{1,0:T(8,128)}) %reduce-scatter.2.cloned.1.call-update) | async-done | bytes 65552 | tf_op jit(solution)/shard_map/reduce_scatter | solution.py:130
  556.7 75.3 %psum.21 = bf16[64,256]{1,0:T(8,128)(2,1)S(1)} all-reduce(bf16[64,256]{1,0:T(8,128)(2,1)S(1)} %convert_element_type.112), channel_id=1, replica_groups=mesh['grp'=8,'tile'=64] {'grp'}, use_global_device_ids=true, to_apply=%region_1.2 | all-reduce | flops 16384 | bytes 65536 | tf_op jit(solution)/shard_map/psum | solution.py:131
  (89 shorter events, 7.3 us)
Async XLA Ops:
  7.2 140.5 %all-gather.2.cloned.1.call-start = ((), (), s32[]{:S(2)}) async-start(), calls=%async_computation.1 | async-start | bytes 2129920 | tf_op jit(solution)/shard_map/all_gather | solution.py:99
  7.9 548.0 %reduce-scatter.2.cloned.1.call-start = ((), (), s32[]{:S(2)}) async-start(), calls=%async_computation.2 | async-start | bytes 4259840 | tf_op jit(solution)/shard_map/reduce_scatter | solution.py:130
  9.1 13.2 %collective-permute-start.1 = (bf16[1,8,128,128]{2,3,1,0:T(8,128)(2,1)S(1)}, bf16[1,8,128,128]{2,3,1,0:T(8,128)(2,1)S(1)}, u32[]{:S(2)}, u32[]{:S(2)}) collective-permute-start(bf16[1,8,128,128]{2,3,1,0:T(8,128)(2,1)S(1)} %copy.11), channel_id=1, source_target_pairs={{64,0},{128,64},{192,128},{256,192},{320,256},{384,320},{448,384},... | collective-permute-start | bytes 786440 | tf_op jit(solution)/shard_map/ppermute | solution.py:17
  17.9 5.2 collective-permute-start
  22.1 128.7 %copy-start.5 = (f32[128]{0:T(128)}, f32[128]{0:T(128)S(1)}, u32[]{:S(2)}) copy-start(f32[128]{0:T(128)S(1)} %get-tuple-element.35) | copy-start | bytes 1540
  22.1 128.7 %copy-start.7 = (f32[128]{0:T(128)}, f32[128]{0:T(128)S(1)}, u32[]{:S(2)}) copy-start(f32[128]{0:T(128)S(1)} %get-tuple-element.36) | copy-start | bytes 1540
  22.1 128.7 %copy-start.9 = (f32[128]{0:T(128)}, f32[128]{0:T(128)S(1)}, u32[]{:S(2)}) copy-start(f32[128]{0:T(128)S(1)} %get-tuple-element.37) | copy-start | bytes 1540
  22.1 128.7 %copy-start.11 = (f32[128]{0:T(128)}, f32[128]{0:T(128)S(1)}, u32[]{:S(2)}) copy-start(f32[128]{0:T(128)S(1)} %get-tuple-element.38) | copy-start | bytes 1540
  22.1 128.7 %copy-start.13 = (f32[128]{0:T(128)}, f32[128]{0:T(128)S(1)}, u32[]{:S(2)}) copy-start(f32[128]{0:T(128)S(1)} %get-tuple-element.39) | copy-start | bytes 1540
  22.1 128.7 %copy-start.15 = (f32[128]{0:T(128)}, f32[128]{0:T(128)S(1)}, u32[]{:S(2)}) copy-start(f32[128]{0:T(128)S(1)} %get-tuple-element.40) | copy-start | bytes 1540
  22.1 128.7 %copy-start.17 = (f32[128]{0:T(128)}, f32[128]{0:T(128)S(1)}, u32[]{:S(2)}) copy-start(f32[128]{0:T(128)S(1)} %get-tuple-element.41) | copy-start | bytes 1540
  22.1 128.7 %copy-start.19 = (f32[128]{0:T(128)}, f32[128]{0:T(128)S(1)}, u32[]{:S(2)}) copy-start(f32[128]{0:T(128)S(1)} %get-tuple-element.42) | copy-start | bytes 1540
  22.2 128.7 %copy-start.21 = (f32[128]{0:T(128)}, f32[128]{0:T(128)S(1)}, u32[]{:S(2)}) copy-start(f32[128]{0:T(128)S(1)} %get-tuple-element.43) | copy-start | bytes 1540
  23.1 127.7 %collective-permute-start.3 = (bf16[3,1,128,128]{2,3,1,0:T(8,128)(2,1)S(1)}, bf16[3,1,128,128]{2,3,1,0:T(8,128)(2,1)S(1)}, u32[]{:S(2)}, u32[]{:S(2)}) collective-permute-start(bf16[3,1,128,128]{2,3,1,0:T(8,128)(2,1)S(1)} %get-tuple-element.24), channel_id=1, source_target_pairs={{1,0},{2,1},{3,2},{4,3},{5,4},{6,5},{7,6},{8,7},{9,8},{10,9},{11,1... | collective-permute-start | bytes 294920 | tf_op jit(solution)/shard_map/ppermute | solution.py:17
  24.4 126.4 %collective-permute-start.2 = (bf16[3,1,128,128]{2,3,1,0:T(8,128)(2,1)S(1)}, bf16[3,1,128,128]{2,3,1,0:T(8,128)(2,1)S(1)}, u32[]{:S(2)}, u32[]{:S(2)}) collective-permute-start(bf16[3,1,128,128]{2,3,1,0:T(8,128)(2,1)S(1)} %get-tuple-element.25), channel_id=1, source_target_pairs={{0,1},{1,2},{2,3},{3,4},{4,5},{5,6},{6,7},{7,8},{8,9},{9,10},{10,1... | collective-permute-start | bytes 294920 | tf_op jit(solution)/shard_map/ppermute | solution.py:14
  155.5 115.4 %collective-permute-start.5 = (bf16[1,8,128,128]{2,3,1,0:T(8,128)(2,1)S(1)}, bf16[1,8,128,128]{2,3,1,0:T(8,128)(2,1)}, u32[]{:S(2)}, u32[]{:S(2)}) collective-permute-start(bf16[1,8,128,128]{2,3,1,0:T(8,128)(2,1)S(1)} %bitcast.128), channel_id=1, source_target_pairs={{64,0},{128,64},{192,128},{256,192},{320,256},{384,320},{448,384},... | collective-permute-start | bytes 786440 | tf_op jit(solution)/shard_map/ppermute | solution.py:17
  161.9 109.0 %collective-permute-start.4 = (bf16[1,8,128,128]{2,3,1,0:T(8,128)(2,1)S(1)}, bf16[1,8,128,128]{2,3,1,0:T(8,128)(2,1)}, u32[]{:S(2)}, u32[]{:S(2)}) collective-permute-start(bf16[1,8,128,128]{2,3,1,0:T(8,128)(2,1)S(1)} %bitcast.129), channel_id=1, source_target_pairs={{0,64},{64,128},{128,192},{192,256},{256,320},{320,384},{384,448},... | collective-permute-start | bytes 786440 | tf_op jit(solution)/shard_map/ppermute | solution.py:14
  169.6 109.2 %copy-start.6 = (f32[128]{0:T(128)S(1)}, f32[128]{0:T(128)}, u32[]{:S(2)}) copy-start(f32[128]{0:T(128)} %copy-done.5) | copy-start | bytes 1540
  169.6 109.2 %copy-start.8 = (f32[128]{0:T(128)S(1)}, f32[128]{0:T(128)}, u32[]{:S(2)}) copy-start(f32[128]{0:T(128)} %copy-done.7) | copy-start | bytes 1540
  169.6 109.2 %copy-start.10 = (f32[128]{0:T(128)S(1)}, f32[128]{0:T(128)}, u32[]{:S(2)}) copy-start(f32[128]{0:T(128)} %copy-done.9) | copy-start | bytes 1540
  169.6 109.2 %copy-start.12 = (f32[128]{0:T(128)S(1)}, f32[128]{0:T(128)}, u32[]{:S(2)}) copy-start(f32[128]{0:T(128)} %copy-done.11) | copy-start | bytes 1540
  169.7 109.2 %copy-start.14 = (f32[128]{0:T(128)S(1)}, f32[128]{0:T(128)}, u32[]{:S(2)}) copy-start(f32[128]{0:T(128)} %copy-done.13) | copy-start | bytes 1540
  271.8 5.8 collective-permute-start.6
  273.1 5.8 collective-permute-start.7
  (13 other events, 466.0 us)
Sparse Core Ops, SparseCore 0:
  12.6 135.0 all-gather.1
  155.6 400.1 reduce-scatter.1
where the time goes:
time: 640 us; the launch traced here: 639 us
  waiting for transfers between devices  396 us (62%)
  blocking collectives  173 us (27%)
  starting transfers between devices  32.8 us (5%)
  between operations  14.6 us (2%)
  matrix products  12.4 us (2%)
    reduce_scatter x1, waiting for transfers between devices, local(): lax.psum_scatter(weight_term, 'tile', scatter_dimension=0, tiled=True)  274 us
    all_gather x1, waiting for transfers between devices, local(): whole_w = lax.all_gather(spectral_w, 'tile', axis=0, tiled=True)  119 us
    psum x1, blocking collectives, local(): conv_all, proj_all = lax.psum((conv_part, proj_grad), ('grp', 'tile'))  97.4 us
    psum x1, blocking collectives, local(): lax.psum(tile_share.astype(jnp.bfloat16), 'grp').astype(jnp.float32)  75.3 us
    ppermute x4, starting transfers between devices, padded(): lax.ppermute(lax.slice_in_dim(block, 0, width, axis=dim), axis, backward)  17.8 us
    ppermute x4, starting transfers between devices, padded(): lax.ppermute(lax.slice_in_dim(block, block.shape[dim] - width, None, axis...  15 us
  transfers between devices with their start and end apart: 10, of which 5 were waited for; matrix products, arithmetic and copies ran while one was open for 3% of the time, Pallas kernels for 0%

commit v1 on v0

--- a/solution.py
+++ b/solution.py
@@ -96,7 +96,9 @@
     for index_d, (row_off, col_off) in enumerate(offsets):
         window = x_pad[1 + row_off : 1 + row_off + rows_here, 1 + col_off : 1 + col_off + cols_here]
         local_term = local_term + window.astype(jnp.float32) * conv_k[index_d]
-    whole_w = lax.all_gather(spectral_w, "tile", axis=0, tiled=True)
+    whole_w = jnp.concatenate(
+        lax.all_to_all(jnp.stack([spectral_w] * lax.axis_size("tile")), "tile", 0, 0), axis=0
+    )
     mixer = build_mixer(whole_w, modes, chans)
     grad_pre, grad_in, weight_term, proj_grad = cell_backward(
         hidden.reshape(cell_count, bins_here, chans),

time: 640 us -> 586 us (0.916)
  waiting for transfers between devices: 396 us -> 317 us
  blocking collectives: 173 us -> 184 us
  starting transfers between devices: 32.8 us -> 43.8 us
    all_gather x1 -> x0, waiting for transfers between devices: 119 us -> none  [local(): whole_w = lax.all_gather(spectral_w, 'tile', axis=0, tiled=True)]
    ppermute x4, waiting for transfers between devices: 0.45 us -> 44.1 us  [padded(): lax.ppermute(lax.slice_in_dim(block, 0, width, axis=dim), axis, backward)]
    all_to_all x0 -> x1, starting transfers between devices: none -> 19.6 us  [local(): lax.all_to_all(jnp.stack([spectral_w] * lax.axis_size('tile')), 'tile', 0...]
    psum x1, blocking collectives: 97.4 us -> 109 us  [local(): conv_all, proj_all = lax.psum((conv_part, proj_grad), ('grp', 'tile'))]
    ppermute x4, starting transfers between devices: 17.8 us -> 7.36 us  [padded(): lax.ppermute(lax.slice_in_dim(block, 0, width, axis=dim), axis, backward)]
  transfers between devices with their start and end apart: 10 -> 10, of which waited for: 5 -> 4; matrix products, arithmetic and copies ran while one was open for 3% -> 3% of each run, Pallas kernels for 0% -> 0%
where the time goes in v1:
time: 586 us; the launch traced here: 585 us
  waiting for transfers between devices  317 us (54%)
  blocking collectives  184 us (31%)
  starting transfers between devices  43.8 us (7%)
  between operations  14.7 us (3%)
  matrix products  12.4 us (2%)
  other arithmetic  7.31 us (1%)
    reduce_scatter x1, waiting for transfers between devices, local(): lax.psum_scatter(weight_term, 'tile', scatter_dimension=0, tiled=True)  272 us
    psum x1, blocking collectives, local(): conv_all, proj_all = lax.psum((conv_part, proj_grad), ('grp', 'tile'))  109 us
    psum x1, blocking collectives, local(): lax.psum(tile_share.astype(jnp.bfloat16), 'grp').astype(jnp.float32)  75.9 us
    ppermute x4, waiting for transfers between devices, padded(): lax.ppermute(lax.slice_in_dim(block, 0, width, axis=dim), axis, backward)  44.1 us
    all_to_all x1, starting transfers between devices, local(): lax.all_to_all(jnp.stack([spectral_w] * lax.axis_size('tile')), 'tile', 0...  19.6 us
    ppermute x4, starting transfers between devices, padded(): lax.ppermute(lax.slice_in_dim(block, block.shape[dim] - width, None, axis...  16.8 us
  transfers between devices with their start and end apart: 10, of which 4 were waited for; matrix products, arithmetic and copies ran while one was open for 3% of the time, Pallas kernels for 0%

profile of v1, /device:TPU:1, one launch (start us, length us, event | category | flops | bytes accessed | tf_op | source)
XLA Modules:
  0.0 585.1 jit_solution(6424242730201914376)
XLA Ops:
  7.2 2.4 stack.22
  9.6 19.6 %all-to-all-start = ((bf16[64,64,256]{2,1,0:T(8,128)(2,1)}), bf16[64,64,256]{2,1,0:T(8,128)(2,1)S(1)}, u32[]{:S(2)}, u32[]{:S(2)}) async-start(bf16[64,64,256]{2,1,0:T(8,128)(2,1)} %stack.22), calls=%async_computation | async-start | bytes 4194304 | tf_op jit(solution)/shard_map/all_to_all | solution.py:100
  29.4 2.9 collective-permute-start.1
  32.3 2.7 collective-permute-start
  37.3 43.7 %collective-permute-done.1 = bf16[1,8,128,128]{2,3,1,0:T(8,128)(2,1)S(1)} collective-permute-done((bf16[1,8,128,128]{2,3,1,0:T(8,128)(2,1)S(1)}, bf16[1,8,128,128]{2,3,1,0:T(8,128)(2,1)S(1)}, u32[]{:S(2)}, u32[]{:S(2)}) %collective-permute-start.1) | collective-permute-done | bytes 262176 | tf_op jit(solution)/shard_map/ppermute | solution.py:17
  81.8 1.3 collective-permute-start.3
  83.1 6.3 %collective-permute-start.2 = (bf16[3,1,128,128]{2,3,1,0:T(8,128)(2,1)}, bf16[3,1,128,128]{2,3,1,0:T(8,128)(2,1)}, u32[]{:S(2)}, u32[]{:S(2)}) collective-permute-start(bf16[3,1,128,128]{2,3,1,0:T(8,128)(2,1)} %get-tuple-element.25), channel_id=1, source_target_pairs={{0,1},{1,2},{2,3},{3,4},{4,5},{5,6},{6,7},{7,8},{8,9},{9,10},{10,1... | collective-permute-start | bytes 294920 | tf_op jit(solution)/shard_map/ppermute | solution.py:14
  90.0 0.9 fusion.2
  91.4 2.6 bitcast_convert_fusion
  94.4 2.7 fusion.24
  97.1 1.9 collective-permute-start.5
  99.0 3.9 collective-permute-start.4
  103.3 1.0 fusion.14
  104.3 1.2 fusion.15
  105.6 3.1 fusion.3
  109.4 108.6 %all-reduce = (f32[9,128]{1,0:T(8,128)}, f32[128]{0:T(128)}) all-reduce(f32[9,128]{1,0:T(8,128)S(1)} %stack.32, f32[128]{0:T(128)S(1)} %convolution_bitcast_fusion.2), channel_id=1, replica_groups=mesh['grp'=8,'tile'=64] {'grp','tile'}, use_global_device_ids=true, to_apply=%region_2.3 | all-reduce | flops 1280 | bytes 10240 | tf_op jit(solution)/shard_map/psum | solution.py:134
  218.8 1.3 collective-permute-start.6
  220.1 4.0 collective-permute-start.7
  224.6 1.2 collective-permute-done.7
  225.9 2.1 fusion.21
  227.9 1.0 copy.20
  228.9 271.9 %reduce-scatter.2.cloned.1.call-done = f32[64,256]{1,0:T(8,128)} async-done(((f32[4096,256]{1,0:T(8,128)}), f32[64,256]{1,0:T(8,128)}) %reduce-scatter.2.cloned.1.call-update) | async-done | bytes 65552 | tf_op jit(solution)/shard_map/reduce_scatter | solution.py:132
  500.9 0.8 convert_element_type.112
  501.7 75.9 %psum.21 = bf16[64,256]{1,0:T(8,128)(2,1)S(1)} all-reduce(bf16[64,256]{1,0:T(8,128)(2,1)S(1)} %convert_element_type.112), channel_id=1, replica_groups=mesh['grp'=8,'tile'=64] {'grp'}, use_global_device_ids=true, to_apply=%region_1.2 | all-reduce | flops 16384 | bytes 65536 | tf_op jit(solution)/shard_map/psum | solution.py:133
  (105 shorter events, 7.4 us)
Async XLA Ops:
  7.2 22.1 %copy-start = (bf16[1,8,128,128]{3,2,1,0:T(8,128)(2,1)S(1)}, bf16[1,8,128,128]{3,2,1,0:T(8,128)(2,1)}, u32[]{:S(2)}) copy-start(bf16[1,8,128,128]{3,2,1,0:T(8,128)(2,1)} %param.5) | copy-start | bytes 786436
  7.2 28.8 %copy-start.12 = (f32[9,128]{1,0:T(8,128)S(1)}, f32[9,128]{1,0:T(8,128)}, u32[]{:S(2)}) copy-start(f32[9,128]{1,0:T(8,128)} %param.8) | copy-start | bytes 13828
  9.6 79.8 %all-to-all-start = ((bf16[64,64,256]{2,1,0:T(8,128)(2,1)}), bf16[64,64,256]{2,1,0:T(8,128)(2,1)S(1)}, u32[]{:S(2)}, u32[]{:S(2)}) async-start(bf16[64,64,256]{2,1,0:T(8,128)(2,1)} %stack.22), calls=%async_computation | async-start | bytes 4194304 | tf_op jit(solution)/shard_map/all_to_all | solution.py:100
  29.2 471.7 %reduce-scatter.2.cloned.1.call-start = ((), (), s32[]{:S(2)}) async-start(), calls=%async_computation.2 | async-start | bytes 4259840 | tf_op jit(solution)/shard_map/reduce_scatter | solution.py:132
  29.4 51.6 %collective-permute-start.1 = (bf16[1,8,128,128]{2,3,1,0:T(8,128)(2,1)S(1)}, bf16[1,8,128,128]{2,3,1,0:T(8,128)(2,1)S(1)}, u32[]{:S(2)}, u32[]{:S(2)}) collective-permute-start(bf16[1,8,128,128]{2,3,1,0:T(8,128)(2,1)S(1)} %copy.11), channel_id=1, source_target_pairs={{64,0},{128,64},{192,128},{256,192},{320,256},{384,320},{448,384},... | collective-permute-start | bytes 786440 | tf_op jit(solution)/shard_map/ppermute | solution.py:17
  32.3 48.7 %collective-permute-start = (bf16[1,8,128,128]{2,3,1,0:T(8,128)(2,1)S(1)}, bf16[1,8,128,128]{2,3,1,0:T(8,128)(2,1)S(1)}, u32[]{:S(2)}, u32[]{:S(2)}) collective-permute-start(bf16[1,8,128,128]{2,3,1,0:T(8,128)(2,1)S(1)} %copy.11), channel_id=1, source_target_pairs={{0,64},{64,128},{128,192},{192,256},{256,320},{320,384},{384,448},... | collective-permute-start | bytes 786440 | tf_op jit(solution)/shard_map/ppermute | solution.py:14
  81.8 9.2 %collective-permute-start.3 = (bf16[3,1,128,128]{2,3,1,0:T(8,128)(2,1)}, bf16[3,1,128,128]{2,3,1,0:T(8,128)(2,1)}, u32[]{:S(2)}, u32[]{:S(2)}) collective-permute-start(bf16[3,1,128,128]{2,3,1,0:T(8,128)(2,1)} %get-tuple-element.24), channel_id=1, source_target_pairs={{1,0},{2,1},{3,2},{4,3},{5,4},{6,5},{7,6},{8,7},{9,8},{10,9},{11,1... | collective-permute-start | bytes 294920 | tf_op jit(solution)/shard_map/ppermute | solution.py:17
  83.1 7.9 %collective-permute-start.2 = (bf16[3,1,128,128]{2,3,1,0:T(8,128)(2,1)}, bf16[3,1,128,128]{2,3,1,0:T(8,128)(2,1)}, u32[]{:S(2)}, u32[]{:S(2)}) collective-permute-start(bf16[3,1,128,128]{2,3,1,0:T(8,128)(2,1)} %get-tuple-element.25), channel_id=1, source_target_pairs={{0,1},{1,2},{2,3},{3,4},{4,5},{5,6},{6,7},{7,8},{8,9},{9,10},{10,1... | collective-permute-start | bytes 294920 | tf_op jit(solution)/shard_map/ppermute | solution.py:14
  89.5 4.5 copy-start.7
  94.3 8.6 %copy-start.9 = (f32[128,128,8]{1,0,2:T(8,128)S(1)}, f32[128,128,8]{1,0,2:T(8,128)}, u32[]{:S(2)}) copy-start(f32[128,128,8]{1,0,2:T(8,128)} %get-tuple-element.18) | copy-start | bytes 1572868
  94.4 8.8 %copy-start.1 = (bf16[1,8,128,128]{3,2,1,0:T(8,128)(2,1)S(1)}, bf16[1,8,128,128]{3,2,1,0:T(8,128)(2,1)}, u32[]{:S(2)}) copy-start(bf16[1,8,128,128]{3,2,1,0:T(8,128)(2,1)} %param.5) | copy-start | bytes 786436
  97.1 120.9 %collective-permute-start.5 = (bf16[1,8,128,128]{2,3,1,0:T(8,128)(2,1)S(1)}, bf16[1,8,128,128]{2,3,1,0:T(8,128)(2,1)}, u32[]{:S(2)}, u32[]{:S(2)}) collective-permute-start(bf16[1,8,128,128]{2,3,1,0:T(8,128)(2,1)S(1)} %bitcast.130), channel_id=1, source_target_pairs={{64,0},{128,64},{192,128},{256,192},{320,256},{384,320},{448,384},... | collective-permute-start | bytes 786440 | tf_op jit(solution)/shard_map/ppermute | solution.py:17
  99.0 119.0 %collective-permute-start.4 = (bf16[1,8,128,128]{2,3,1,0:T(8,128)(2,1)S(1)}, bf16[1,8,128,128]{2,3,1,0:T(8,128)(2,1)}, u32[]{:S(2)}, u32[]{:S(2)}) collective-permute-start(bf16[1,8,128,128]{2,3,1,0:T(8,128)(2,1)S(1)} %bitcast.131), channel_id=1, source_target_pairs={{0,64},{64,128},{128,192},{192,256},{256,320},{320,384},{384,448},... | collective-permute-start | bytes 786440 | tf_op jit(solution)/shard_map/ppermute | solution.py:14
  105.5 120.3 %copy-start.14 = (f32[128]{0:T(128)S(1)}, f32[128]{0:T(128)}, u32[]{:S(2)}) copy-start(f32[128]{0:T(128)} %get-tuple-element.35) | copy-start | bytes 1540
  105.5 120.3 %copy-start.16 = (f32[128]{0:T(128)S(1)}, f32[128]{0:T(128)}, u32[]{:S(2)}) copy-start(f32[128]{0:T(128)} %get-tuple-element.36) | copy-start | bytes 1540
  105.5 120.3 %copy-start.18 = (f32[128]{0:T(128)S(1)}, f32[128]{0:T(128)}, u32[]{:S(2)}) copy-start(f32[128]{0:T(128)} %get-tuple-element.37) | copy-start | bytes 1540
  105.5 120.3 %copy-start.20 = (f32[128]{0:T(128)S(1)}, f32[128]{0:T(128)}, u32[]{:S(2)}) copy-start(f32[128]{0:T(128)} %get-tuple-element.38) | copy-start | bytes 1540
  105.5 120.3 %copy-start.22 = (f32[128]{0:T(128)S(1)}, f32[128]{0:T(128)}, u32[]{:S(2)}) copy-start(f32[128]{0:T(128)} %get-tuple-element.39) | copy-start | bytes 1540
  105.6 120.3 %copy-start.24 = (f32[128]{0:T(128)S(1)}, f32[128]{0:T(128)}, u32[]{:S(2)}) copy-start(f32[128]{0:T(128)} %get-tuple-element.40) | copy-start | bytes 1540
  105.6 120.3 %copy-start.26 = (f32[128]{0:T(128)S(1)}, f32[128]{0:T(128)}, u32[]{:S(2)}) copy-start(f32[128]{0:T(128)} %get-tuple-element.41) | copy-start | bytes 1540
  105.6 120.3 %copy-start.28 = (f32[128]{0:T(128)S(1)}, f32[128]{0:T(128)}, u32[]{:S(2)}) copy-start(f32[128]{0:T(128)} %get-tuple-element.42) | copy-start | bytes 1540
  105.6 120.3 %copy-start.30 = (f32[128]{0:T(128)S(1)}, f32[128]{0:T(128)}, u32[]{:S(2)}) copy-start(f32[128]{0:T(128)} %get-tuple-element.43) | copy-start | bytes 1540
  218.8 5.8 collective-permute-start.6
  220.1 5.7 collective-permute-start.7
  (21 other events, 38.5 us)
Sparse Core Ops, SparseCore 0:
  97.2 403.6 reduce-scatter.1
